TPU v7x, 32 devices: a whole 2x2x4 slice. The times are simulated.
32 devices in a mesh: blk: 8 (over z, x), narrow: 4 (over y, core).
Axes of the slice: x: 2, y: 2, z: 4, core: 2. Of those that a mesh axis runs over, the one named last changes fastest.
Arguments:
- source: float32 [1024, 32, 128], P('blk', 'narrow'), may hold values from -6 to 6
- shift: float32 [1024, 32, 128], P('blk', 'narrow'), may hold values from 0.05 to 1
- start_field: float32 [1024, 32, 128], P('blk', 'narrow'), may hold values from -6 to 6
Outputs:
- field: float32 [1024, 32, 128], P('blk', 'narrow')
All inputs are finite; a program needn't handle non-finite values.
Results may differ from a plain program's by a relative error of at most 0.0003.
Values sent between devices are 32-bit elements; how exact they have to be, the bound alone decides.
A program may use at most 64 MiB of HBM per device.

v0:
```python
import jax
import jax.numpy as jnp
from jax import lax
from jax.sharding import PartitionSpec as P

OV = 8
PASSES = 3
SWEEPS = 2


low_end = 0.05
high_end = 2.2
centre_weight = 1.0 + 1.0 / 7.0


def extended(cells, sides, width, closed):
    for axis, dim in sides:
        count = lax.axis_size(axis)
        ends = count if closed else count - 1
        head = lax.slice_in_dim(cells, 0, width, axis=dim)
        tail = lax.slice_in_dim(cells, cells.shape[dim] - width, cells.shape[dim], axis=dim)
        cells = jnp.concatenate(
            [
                lax.ppermute(tail, axis, [(i, (i + 1) % count) for i in range(ends)]),
                cells,
                lax.ppermute(head, axis, [((i + 1) % count, i) for i in range(ends)]),
            ],
            axis=dim,
        )
    return cells


def passed_along(block, axis, distance):
    devices = range(lax.axis_size(axis))
    route = [((i - distance) % len(devices), i) for i in devices]
    return lax.ppermute(block, axis, route)


def cheby_terms(passes):
    centre = (high_end + low_end) / 2.0
    half_width = (high_end - low_end) / 2.0
    sigma_value = centre / half_width
    ratio_now = 1.0 / sigma_value
    terms = []
    for repeat in range(passes):
        ratio_next = 1.0 / (2.0 * sigma_value - ratio_now)
        terms.append((ratio_next * ratio_now, 2.0 * ratio_next / half_width))
        ratio_now = ratio_next
    return (centre, terms)


def smooth(padded):
    along_x = 0.5 * (padded[:-2] + padded[2:]) + padded[1:-1]
    along_y = 0.5 * (along_x[:, :-2] + along_x[:, 2:]) + along_x[:, 1:-1]
    return 0.5 * (along_y[:, :, :-2] + along_y[:, :, 2:]) + along_y[:, :, 1:-1]


def operate(padded, shift):
    inner = padded[1:-1, 1:-1, 1:-1]
    return (centre_weight + shift) * inner - smooth(padded) / 7.0


def sides(field):
    return extended(field, (("narrow", 1),), 1, False)


def pad_depth(field):
    return jnp.pad(field, ((0, 0), (0, 0), (1, 1)))


def pad_ends(field):
    return jnp.pad(field, ((1, 1), (0, 0), (1, 1)))


def per_device(source, shift, start_field):
    cells_x, cells_y, cells_z = source.shape
    margin = OV
    place = lax.axis_index("blk")
    centre, terms = cheby_terms(PASSES)
    shift_wide = extended(shift, (("blk", 0),), margin, True)
    field = start_field
    for sweep in range(SWEEPS):
        for colour in range(2):
            state_wide = extended(field, (("blk", 0),), 1, True)
            owned_residue = source - operate(pad_depth(sides(state_wide)), shift)
            residue = extended(owned_residue, (("blk", 0),), margin, True)
            direction = residue / centre
            update = direction
            for scale_old, scale_new in terms:
                image = operate(pad_ends(sides(direction)), shift_wide)
                residue = residue - image
                direction = scale_old * direction + scale_new * residue
                update = update + direction
            active = (place % 2 == colour).astype(jnp.float32)
            update = update * active
            from_below = passed_along(update[margin + cells_x :], "blk", 1)
            from_above = passed_along(update[:margin], "blk", -1)
            field = field + update[margin : margin + cells_x]
            field = field.at[:margin].add(from_below)
            field = field.at[cells_x - margin :].add(from_above)
    return field


def solution(mesh):
    placed = (P("blk", "narrow", None), P("blk", "narrow", None), P("blk", "narrow", None))
    return jax.shard_map(
        per_device, mesh=mesh, in_specs=placed, out_specs=P("blk", "narrow", None), check_vma=False
    )
```

profile of v0, /device:TPU:1, one launch (start us, length us, event | category | flops | bytes accessed | tf_op | source)
XLA Modules:
  0.0 260.2 jit_solution(1788768811261481912)
XLA Ops:
  0.7 5.1 %collective-permute-start.1 = (f32[1,8,128]{2,0,1:T(1,128)S(1)}, f32[1,8,128]{2,0,1:T(1,128)S(1)}, u32[]{:S(2)}, u32[]{:S(2)}) collective-permute-start(f32[1,8,128]{2,0,1:T(1,128)S(1)} %bitcast.3), channel_id=1, source_target_pairs={{4,0},{8,4},{12,8},{16,12},{20,16},{24,20},{28,24},{0,28},{5,1},{9... | collective-permute-start | bytes 12296 | tf_op jit(solution)/shard_map/ppermute | solution.py:26
  6.9 4.0 %collective-permute-done = f32[1,8,128]{2,0,1:T(1,128)S(1)} collective-permute-done((f32[1,8,128]{2,0,1:T(1,128)S(1)}, f32[1,8,128]{2,0,1:T(1,128)S(1)}, u32[]{:S(2)}, u32[]{:S(2)}) %collective-permute-start) | collective-permute-done | bytes 4128 | tf_op jit(solution)/shard_map/ppermute | solution.py:24
  11.0 5.1 %collective-permute-start.2 = (f32[130,1,128]{2,0,1:T(8,128)S(1)}, f32[130,1,128]{2,0,1:T(8,128)S(1)}, u32[]{:S(2)}, u32[]{:S(2)}) collective-permute-start(f32[130,1,128]{2,0,1:T(8,128)S(1)} %get-tuple-element.153), channel_id=1, source_target_pairs={{0,1},{1,2},{2,3},{4,5},{5,6},{6,7},{8,9},{9,10},{10,11},{12,13},{... | collective-permute-start | bytes 199688 | tf_op jit(solution)/shard_map/ppermute | solution.py:24
  16.1 1.9 collective-permute-start.3
  18.0 3.7 %collective-permute-done.3 = f32[130,1,128]{2,0,1:T(8,128)S(1)} collective-permute-done((f32[130,1,128]{2,0,1:T(8,128)S(1)}, f32[130,1,128]{2,0,1:T(8,128)S(1)}, u32[]{:S(2)}, u32[]{:S(2)}) %collective-permute-start.3) | collective-permute-done | bytes 66592 | tf_op jit(solution)/shard_map/ppermute | solution.py:26
  24.4 4.1 %collective-permute-start.5 = (f32[8,8,128]{2,0,1:T(8,128)S(1)}, f32[8,8,128]{2,0,1:T(8,128)S(1)}, u32[]{:S(2)}, u32[]{:S(2)}) collective-permute-start(f32[8,8,128]{2,0,1:T(8,128)S(1)} %get-tuple-element.166), channel_id=1, source_target_pairs={{4,0},{8,4},{12,8},{16,12},{20,16},{24,20},{28,24},{0,28},{5,1},{9... | collective-permute-start | bytes 98312 | tf_op jit(solution)/shard_map/ppermute | solution.py:26
  29.9 3.0 %collective-permute-start.8 = (f32[144,1,128]{2,0,1:T(8,128)S(1)}, f32[144,1,128]{2,0,1:T(8,128)S(1)}, u32[]{:S(2)}, u32[]{:S(2)}) collective-permute-start(f32[144,1,128]{2,0,1:T(8,128)S(1)} %get-tuple-element.145), channel_id=1, source_target_pairs={{0,1},{1,2},{2,3},{4,5},{5,6},{6,7},{8,9},{9,10},{10,11},{12,13},{... | collective-permute-start | bytes 221192 | tf_op jit(solution)/shard_map/ppermute | solution.py:24
  32.9 1.9 collective-permute-start.9
  34.9 4.5 %collective-permute-start.7 = (f32[8,8,128]{2,0,1:T(8,128)S(1)}, f32[8,8,128]{2,0,1:T(8,128)S(1)}, u32[]{:S(2)}, u32[]{:S(2)}) collective-permute-start(f32[8,8,128]{2,0,1:T(8,128)S(1)} %get-tuple-element.162), channel_id=1, source_target_pairs={{4,0},{8,4},{12,8},{16,12},{20,16},{24,20},{28,24},{0,28},{5,1},{9... | collective-permute-start | bytes 98312 | tf_op jit(solution)/shard_map/ppermute | solution.py:26
  41.1 4.5 %collective-permute-start.10 = (f32[144,1,128]{2,0,1:T(8,128)S(1)}, f32[144,1,128]{2,0,1:T(8,128)S(1)}, u32[]{:S(2)}, u32[]{:S(2)}) collective-permute-start(f32[144,1,128]{2,0,1:T(8,128)S(1)} %get-tuple-element.143), channel_id=1, source_target_pairs={{0,1},{1,2},{2,3},{4,5},{5,6},{6,7},{8,9},{9,10},{10,11},{12,13},{... | collective-permute-start | bytes 221192 | tf_op jit(solution)/shard_map/ppermute | solution.py:24
  45.6 1.9 collective-permute-start.11
  47.6 3.7 %collective-permute-done.11 = f32[144,1,128]{2,0,1:T(8,128)S(1)} collective-permute-done((f32[144,1,128]{2,0,1:T(8,128)S(1)}, f32[144,1,128]{2,0,1:T(8,128)S(1)}, u32[]{:S(2)}, u32[]{:S(2)}) %collective-permute-start.11) | collective-permute-done | bytes 73760 | tf_op jit(solution)/shard_map/ppermute | solution.py:26
  53.4 1.9 collective-permute-start.12
  55.3 2.4 collective-permute-start.13
  57.7 3.5 %collective-permute-done.13 = f32[144,1,128]{2,0,1:T(8,128)} collective-permute-done((f32[144,1,128]{2,0,1:T(8,128)}, f32[144,1,128]{2,0,1:T(8,128)}, u32[]{:S(2)}, u32[]{:S(2)}) %collective-permute-start.13) | collective-permute-done | bytes 73760 | tf_op jit(solution)/shard_map/ppermute | solution.py:26
  65.2 4.6 %collective-permute-start.15 = (f32[8,8,128]{2,0,1:T(8,128)S(1)}, f32[8,8,128]{2,0,1:T(8,128)S(1)}, u32[]{:S(2)}, u32[]{:S(2)}) collective-permute-start(f32[8,8,128]{2,0,1:T(8,128)S(1)} %get-tuple-element.139), channel_id=1, source_target_pairs={{4,0},{8,4},{12,8},{16,12},{20,16},{24,20},{28,24},{0,28},{5,1},{9... | collective-permute-start | bytes 98312 | tf_op jit(solution)/shard_map/ppermute | solution.py:36
  70.8 4.5 %collective-permute-start.17 = (f32[1,8,128]{2,0,1:T(1,128)S(1)}, f32[1,8,128]{2,0,1:T(1,128)S(1)}, u32[]{:S(2)}, u32[]{:S(2)}) collective-permute-start(f32[1,8,128]{2,0,1:T(1,128)S(1)} %slice.1115), channel_id=1, source_target_pairs={{4,0},{8,4},{12,8},{16,12},{20,16},{24,20},{28,24},{0,28},{5,1},{9... | collective-permute-start | bytes 12296 | tf_op jit(solution)/shard_map/ppermute | solution.py:26
  76.1 4.6 %collective-permute-done.16 = f32[1,8,128]{2,0,1:T(1,128)S(1)} collective-permute-done((f32[1,8,128]{2,0,1:T(1,128)S(1)}, f32[1,8,128]{2,0,1:T(1,128)S(1)}, u32[]{:S(2)}, u32[]{:S(2)}) %collective-permute-start.16) | collective-permute-done | bytes 4128 | tf_op jit(solution)/shard_map/ppermute | solution.py:24
  80.7 4.2 %collective-permute-start.18 = (f32[130,1,128]{2,0,1:T(8,128)S(1)}, f32[130,1,128]{2,0,1:T(8,128)S(1)}, u32[]{:S(2)}, u32[]{:S(2)}) collective-permute-start(f32[130,1,128]{2,0,1:T(8,128)S(1)} %get-tuple-element.151), channel_id=1, source_target_pairs={{0,1},{1,2},{2,3},{4,5},{5,6},{6,7},{8,9},{9,10},{10,11},{12,13},{... | collective-permute-start | bytes 199688 | tf_op jit(solution)/shard_map/ppermute | solution.py:24
  84.9 1.9 collective-permute-start.19
  86.9 3.7 %collective-permute-done.19 = f32[130,1,128]{2,0,1:T(8,128)S(1)} collective-permute-done((f32[130,1,128]{2,0,1:T(8,128)S(1)}, f32[130,1,128]{2,0,1:T(8,128)S(1)}, u32[]{:S(2)}, u32[]{:S(2)}) %collective-permute-start.19) | collective-permute-done | bytes 66592 | tf_op jit(solution)/shard_map/ppermute | solution.py:26
  92.8 4.1 %collective-permute-start.21 = (f32[8,8,128]{2,0,1:T(8,128)S(1)}, f32[8,8,128]{2,0,1:T(8,128)S(1)}, u32[]{:S(2)}, u32[]{:S(2)}) collective-permute-start(f32[8,8,128]{2,0,1:T(8,128)S(1)} %get-tuple-element.160), channel_id=1, source_target_pairs={{4,0},{8,4},{12,8},{16,12},{20,16},{24,20},{28,24},{0,28},{5,1},{9... | collective-permute-start | bytes 98312 | tf_op jit(solution)/shard_map/ppermute | solution.py:26
  98.4 3.0 %collective-permute-start.22 = (f32[144,1,128]{2,0,1:T(8,128)S(1)}, f32[144,1,128]{2,0,1:T(8,128)S(1)}, u32[]{:S(2)}, u32[]{:S(2)}) collective-permute-start(f32[144,1,128]{2,0,1:T(8,128)S(1)} %get-tuple-element.137), channel_id=1, source_target_pairs={{0,1},{1,2},{2,3},{4,5},{5,6},{6,7},{8,9},{9,10},{10,11},{12,13},{... | collective-permute-start | bytes 221192 | tf_op jit(solution)/shard_map/ppermute | solution.py:24
  101.4 1.9 collective-permute-start.23
  103.3 3.7 %collective-permute-done.23 = f32[144,1,128]{2,0,1:T(8,128)S(1)} collective-permute-done((f32[144,1,128]{2,0,1:T(8,128)S(1)}, f32[144,1,128]{2,0,1:T(8,128)S(1)}, u32[]{:S(2)}, u32[]{:S(2)}) %collective-permute-start.23) | collective-permute-done | bytes 73760 | tf_op jit(solution)/shard_map/ppermute | solution.py:26
  108.5 1.9 collective-permute-start.24
  110.4 2.6 collective-permute-start.25
  113.0 3.1 %collective-permute-done.25 = f32[144,1,128]{2,0,1:T(8,128)S(1)} collective-permute-done((f32[144,1,128]{2,0,1:T(8,128)S(1)}, f32[144,1,128]{2,0,1:T(8,128)S(1)}, u32[]{:S(2)}, u32[]{:S(2)}) %collective-permute-start.25) | collective-permute-done | bytes 73760 | tf_op jit(solution)/shard_map/ppermute | solution.py:26
  119.0 1.9 collective-permute-start.26
  120.9 2.4 collective-permute-start.27
  123.3 3.5 %collective-permute-done.27 = f32[144,1,128]{2,0,1:T(8,128)S(1)} collective-permute-done((f32[144,1,128]{2,0,1:T(8,128)}, f32[144,1,128]{2,0,1:T(8,128)S(1)}, u32[]{:S(2)}, u32[]{:S(2)}) %collective-permute-start.27) | collective-permute-done | bytes 73760 | tf_op jit(solution)/shard_map/ppermute | solution.py:26
  130.7 4.5 %collective-permute-start.29 = (f32[8,8,128]{2,0,1:T(8,128)S(1)}, f32[8,8,128]{2,0,1:T(8,128)S(1)}, u32[]{:S(2)}, u32[]{:S(2)}) collective-permute-start(f32[8,8,128]{2,0,1:T(8,128)S(1)} %get-tuple-element.131), channel_id=1, source_target_pairs={{4,0},{8,4},{12,8},{16,12},{20,16},{24,20},{28,24},{0,28},{5,1},{9... | collective-permute-start | bytes 98312 | tf_op jit(solution)/shard_map/ppermute | solution.py:36
  136.4 4.3 %collective-permute-start.31 = (f32[1,8,128]{2,0,1:T(1,128)S(1)}, f32[1,8,128]{2,0,1:T(1,128)S(1)}, u32[]{:S(2)}, u32[]{:S(2)}) collective-permute-start(f32[1,8,128]{2,0,1:T(1,128)S(1)} %slice.1166), channel_id=1, source_target_pairs={{4,0},{8,4},{12,8},{16,12},{20,16},{24,20},{28,24},{0,28},{5,1},{9... | collective-permute-start | bytes 12296 | tf_op jit(solution)/shard_map/ppermute | solution.py:26
  141.5 4.6 %collective-permute-done.30 = f32[1,8,128]{2,0,1:T(1,128)S(1)} collective-permute-done((f32[1,8,128]{2,0,1:T(1,128)S(1)}, f32[1,8,128]{2,0,1:T(1,128)S(1)}, u32[]{:S(2)}, u32[]{:S(2)}) %collective-permute-start.30) | collective-permute-done | bytes 4128 | tf_op jit(solution)/shard_map/ppermute | solution.py:24
  146.1 4.4 %collective-permute-start.32 = (f32[130,1,128]{2,0,1:T(8,128)S(1)}, f32[130,1,128]{2,0,1:T(8,128)S(1)}, u32[]{:S(2)}, u32[]{:S(2)}) collective-permute-start(f32[130,1,128]{2,0,1:T(8,128)S(1)} %get-tuple-element.149), channel_id=1, source_target_pairs={{0,1},{1,2},{2,3},{4,5},{5,6},{6,7},{8,9},{9,10},{10,11},{12,13},{... | collective-permute-start | bytes 199688 | tf_op jit(solution)/shard_map/ppermute | solution.py:24
  150.5 1.9 collective-permute-start.33
  152.4 3.7 %collective-permute-done.33 = f32[130,1,128]{2,0,1:T(8,128)S(1)} collective-permute-done((f32[130,1,128]{2,0,1:T(8,128)S(1)}, f32[130,1,128]{2,0,1:T(8,128)S(1)}, u32[]{:S(2)}, u32[]{:S(2)}) %collective-permute-start.33) | collective-permute-done | bytes 66592 | tf_op jit(solution)/shard_map/ppermute | solution.py:26
  158.4 4.1 %collective-permute-start.35 = (f32[8,8,128]{2,0,1:T(8,128)S(1)}, f32[8,8,128]{2,0,1:T(8,128)S(1)}, u32[]{:S(2)}, u32[]{:S(2)}) collective-permute-start(f32[8,8,128]{2,0,1:T(8,128)S(1)} %get-tuple-element.158), channel_id=1, source_target_pairs={{4,0},{8,4},{12,8},{16,12},{20,16},{24,20},{28,24},{0,28},{5,1},{9... | collective-permute-start | bytes 98312 | tf_op jit(solution)/shard_map/ppermute | solution.py:26
  163.9 3.0 %collective-permute-start.36 = (f32[144,1,128]{2,0,1:T(8,128)S(1)}, f32[144,1,128]{2,0,1:T(8,128)S(1)}, u32[]{:S(2)}, u32[]{:S(2)}) collective-permute-start(f32[144,1,128]{2,0,1:T(8,128)S(1)} %get-tuple-element.129), channel_id=1, source_target_pairs={{0,1},{1,2},{2,3},{4,5},{5,6},{6,7},{8,9},{9,10},{10,11},{12,13},{... | collective-permute-start | bytes 221192 | tf_op jit(solution)/shard_map/ppermute | solution.py:24
  166.9 1.9 collective-permute-start.37
  168.9 3.7 %collective-permute-done.37 = f32[144,1,128]{2,0,1:T(8,128)S(1)} collective-permute-done((f32[144,1,128]{2,0,1:T(8,128)S(1)}, f32[144,1,128]{2,0,1:T(8,128)S(1)}, u32[]{:S(2)}, u32[]{:S(2)}) %collective-permute-start.37) | collective-permute-done | bytes 73760 | tf_op jit(solution)/shard_map/ppermute | solution.py:26
  174.0 1.9 collective-permute-start.38
  175.9 2.4 collective-permute-start.39
  178.4 3.2 %collective-permute-done.39 = f32[144,1,128]{2,0,1:T(8,128)S(1)} collective-permute-done((f32[144,1,128]{2,0,1:T(8,128)S(1)}, f32[144,1,128]{2,0,1:T(8,128)S(1)}, u32[]{:S(2)}, u32[]{:S(2)}) %collective-permute-start.39) | collective-permute-done | bytes 73760 | tf_op jit(solution)/shard_map/ppermute | solution.py:26
  183.0 1.9 collective-permute-start.40
  184.9 2.4 collective-permute-start.41
  187.4 3.2 %collective-permute-done.41 = f32[144,1,128]{2,0,1:T(8,128)S(1)} collective-permute-done((f32[144,1,128]{2,0,1:T(8,128)S(1)}, f32[144,1,128]{2,0,1:T(8,128)S(1)}, u32[]{:S(2)}, u32[]{:S(2)}) %collective-permute-start.41) | collective-permute-done | bytes 73760 | tf_op jit(solution)/shard_map/ppermute | solution.py:26
  192.6 4.5 %collective-permute-start.43 = (f32[8,8,128]{2,0,1:T(8,128)S(1)}, f32[8,8,128]{2,0,1:T(8,128)S(1)}, u32[]{:S(2)}, u32[]{:S(2)}) collective-permute-start(f32[8,8,128]{2,0,1:T(8,128)S(1)} %get-tuple-element.123), channel_id=1, source_target_pairs={{4,0},{8,4},{12,8},{16,12},{20,16},{24,20},{28,24},{0,28},{5,1},{9... | collective-permute-start | bytes 98312 | tf_op jit(solution)/shard_map/ppermute | solution.py:36
  198.3 4.3 %collective-permute-start.45 = (f32[1,8,128]{2,0,1:T(1,128)S(1)}, f32[1,8,128]{2,0,1:T(1,128)S(1)}, u32[]{:S(2)}, u32[]{:S(2)}) collective-permute-start(f32[1,8,128]{2,0,1:T(1,128)S(1)} %slice.1217), channel_id=1, source_target_pairs={{4,0},{8,4},{12,8},{16,12},{20,16},{24,20},{28,24},{0,28},{5,1},{9... | collective-permute-start | bytes 12296 | tf_op jit(solution)/shard_map/ppermute | solution.py:26
  203.4 4.6 %collective-permute-done.44 = f32[1,8,128]{2,0,1:T(1,128)S(1)} collective-permute-done((f32[1,8,128]{2,0,1:T(1,128)S(1)}, f32[1,8,128]{2,0,1:T(1,128)S(1)}, u32[]{:S(2)}, u32[]{:S(2)}) %collective-permute-start.44) | collective-permute-done | bytes 4128 | tf_op jit(solution)/shard_map/ppermute | solution.py:24
  208.0 4.3 %collective-permute-start.46 = (f32[130,1,128]{2,0,1:T(8,128)S(1)}, f32[130,1,128]{2,0,1:T(8,128)S(1)}, u32[]{:S(2)}, u32[]{:S(2)}) collective-permute-start(f32[130,1,128]{2,0,1:T(8,128)S(1)} %get-tuple-element.147), channel_id=1, source_target_pairs={{0,1},{1,2},{2,3},{4,5},{5,6},{6,7},{8,9},{9,10},{10,11},{12,13},{... | collective-permute-start | bytes 199688 | tf_op jit(solution)/shard_map/ppermute | solution.py:24
  212.2 2.1 collective-permute-start.47
  214.4 3.5 %collective-permute-done.47 = f32[130,1,128]{2,0,1:T(8,128)S(1)} collective-permute-done((f32[130,1,128]{2,0,1:T(8,128)S(1)}, f32[130,1,128]{2,0,1:T(8,128)S(1)}, u32[]{:S(2)}, u32[]{:S(2)}) %collective-permute-start.47) | collective-permute-done | bytes 66592 | tf_op jit(solution)/shard_map/ppermute | solution.py:26
  219.2 4.1 %collective-permute-start.49 = (f32[8,8,128]{2,0,1:T(8,128)S(1)}, f32[8,8,128]{2,0,1:T(8,128)S(1)}, u32[]{:S(2)}, u32[]{:S(2)}) collective-permute-start(f32[8,8,128]{2,0,1:T(8,128)S(1)} %get-tuple-element.156), channel_id=1, source_target_pairs={{4,0},{8,4},{12,8},{16,12},{20,16},{24,20},{28,24},{0,28},{5,1},{9... | collective-permute-start | bytes 98312 | tf_op jit(solution)/shard_map/ppermute | solution.py:26
  224.8 3.0 %collective-permute-start.50 = (f32[144,1,128]{2,0,1:T(8,128)S(1)}, f32[144,1,128]{2,0,1:T(8,128)S(1)}, u32[]{:S(2)}, u32[]{:S(2)}) collective-permute-start(f32[144,1,128]{2,0,1:T(8,128)S(1)} %get-tuple-element.121), channel_id=1, source_target_pairs={{0,1},{1,2},{2,3},{4,5},{5,6},{6,7},{8,9},{9,10},{10,11},{12,13},{... | collective-permute-start | bytes 221192 | tf_op jit(solution)/shard_map/ppermute | solution.py:24
  227.8 1.9 collective-permute-start.51
  229.7 3.7 %collective-permute-done.51 = f32[144,1,128]{2,0,1:T(8,128)S(1)} collective-permute-done((f32[144,1,128]{2,0,1:T(8,128)S(1)}, f32[144,1,128]{2,0,1:T(8,128)S(1)}, u32[]{:S(2)}, u32[]{:S(2)}) %collective-permute-start.51) | collective-permute-done | bytes 73760 | tf_op jit(solution)/shard_map/ppermute | solution.py:26
  234.8 1.9 collective-permute-start.52
  236.8 2.4 collective-permute-start.53
  239.2 3.2 %collective-permute-done.53 = f32[144,1,128]{2,0,1:T(8,128)S(1)} collective-permute-done((f32[144,1,128]{2,0,1:T(8,128)S(1)}, f32[144,1,128]{2,0,1:T(8,128)S(1)}, u32[]{:S(2)}, u32[]{:S(2)}) %collective-permute-start.53) | collective-permute-done | bytes 73760 | tf_op jit(solution)/shard_map/ppermute | solution.py:26
  243.9 1.9 collective-permute-start.54
  245.8 2.4 collective-permute-start.55
  248.2 3.2 %collective-permute-done.55 = f32[144,1,128]{2,0,1:T(8,128)S(1)} collective-permute-done((f32[144,1,128]{2,0,1:T(8,128)S(1)}, f32[144,1,128]{2,0,1:T(8,128)S(1)}, u32[]{:S(2)}, u32[]{:S(2)}) %collective-permute-start.55) | collective-permute-done | bytes 73760 | tf_op jit(solution)/shard_map/ppermute | solution.py:26
  253.4 4.5 %collective-permute-start.57 = (f32[8,8,128]{2,0,1:T(8,128)S(1)}, f32[8,8,128]{2,0,1:T(8,128)S(1)}, u32[]{:S(2)}, u32[]{:S(2)}) collective-permute-start(f32[8,8,128]{2,0,1:T(8,128)S(1)} %get-tuple-element.115), channel_id=1, source_target_pairs={{4,0},{8,4},{12,8},{16,12},{20,16},{24,20},{28,24},{0,28},{5,1},{9... | collective-permute-start | bytes 98312 | tf_op jit(solution)/shard_map/ppermute | solution.py:36
  (188 shorter events, 48.7 us)
Async XLA Ops:
  0.7 6.2 %collective-permute-start.1 = (f32[1,8,128]{2,0,1:T(1,128)S(1)}, f32[1,8,128]{2,0,1:T(1,128)S(1)}, u32[]{:S(2)}, u32[]{:S(2)}) collective-permute-start(f32[1,8,128]{2,0,1:T(1,128)S(1)} %bitcast.3), channel_id=1, source_target_pairs={{4,0},{8,4},{12,8},{16,12},{20,16},{24,20},{28,24},{0,28},{5,1},{9... | collective-permute-start | bytes 12296 | tf_op jit(solution)/shard_map/ppermute | solution.py:26
  5.8 5.2 %collective-permute-start = (f32[1,8,128]{2,0,1:T(1,128)S(1)}, f32[1,8,128]{2,0,1:T(1,128)S(1)}, u32[]{:S(2)}, u32[]{:S(2)}) collective-permute-start(f32[1,8,128]{2,0,1:T(1,128)S(1)} %bitcast.2), channel_id=1, source_target_pairs={{0,4},{4,8},{8,12},{12,16},{16,20},{20,24},{24,28},{28,0},{1,5},{5... | collective-permute-start | bytes 12296 | tf_op jit(solution)/shard_map/ppermute | solution.py:24
  11.0 7.1 %collective-permute-start.2 = (f32[130,1,128]{2,0,1:T(8,128)S(1)}, f32[130,1,128]{2,0,1:T(8,128)S(1)}, u32[]{:S(2)}, u32[]{:S(2)}) collective-permute-start(f32[130,1,128]{2,0,1:T(8,128)S(1)} %get-tuple-element.153), channel_id=1, source_target_pairs={{0,1},{1,2},{2,3},{4,5},{5,6},{6,7},{8,9},{9,10},{10,11},{12,13},{... | collective-permute-start | bytes 199688 | tf_op jit(solution)/shard_map/ppermute | solution.py:24
  16.1 5.6 %collective-permute-start.3 = (f32[130,1,128]{2,0,1:T(8,128)S(1)}, f32[130,1,128]{2,0,1:T(8,128)S(1)}, u32[]{:S(2)}, u32[]{:S(2)}) collective-permute-start(f32[130,1,128]{2,0,1:T(8,128)S(1)} %get-tuple-element.154), channel_id=1, source_target_pairs={{1,0},{2,1},{3,2},{5,4},{6,5},{7,6},{9,8},{10,9},{11,10},{13,12},{... | collective-permute-start | bytes 199688 | tf_op jit(solution)/shard_map/ppermute | solution.py:26
  22.5 1.2 copy-start.1
  22.5 1.3 copy-start.8
  24.3 5.5 %collective-permute-start.4 = (f32[8,8,128]{2,0,1:T(8,128)S(1)}, f32[8,8,128]{2,0,1:T(8,128)S(1)}, u32[]{:S(2)}, u32[]{:S(2)}) collective-permute-start(f32[8,8,128]{2,0,1:T(8,128)S(1)} %get-tuple-element.165), channel_id=1, source_target_pairs={{0,4},{4,8},{8,12},{12,16},{16,20},{20,24},{24,28},{28,0},{1,5},{5... | collective-permute-start | bytes 98312 | tf_op jit(solution)/shard_map/ppermute | solution.py:24
  24.4 5.5 %collective-permute-start.5 = (f32[8,8,128]{2,0,1:T(8,128)S(1)}, f32[8,8,128]{2,0,1:T(8,128)S(1)}, u32[]{:S(2)}, u32[]{:S(2)}) collective-permute-start(f32[8,8,128]{2,0,1:T(8,128)S(1)} %get-tuple-element.166), channel_id=1, source_target_pairs={{4,0},{8,4},{12,8},{16,12},{20,16},{24,20},{28,24},{0,28},{5,1},{9... | collective-permute-start | bytes 98312 | tf_op jit(solution)/shard_map/ppermute | solution.py:26
  29.9 9.5 %collective-permute-start.8 = (f32[144,1,128]{2,0,1:T(8,128)S(1)}, f32[144,1,128]{2,0,1:T(8,128)S(1)}, u32[]{:S(2)}, u32[]{:S(2)}) collective-permute-start(f32[144,1,128]{2,0,1:T(8,128)S(1)} %get-tuple-element.145), channel_id=1, source_target_pairs={{0,1},{1,2},{2,3},{4,5},{5,6},{6,7},{8,9},{9,10},{10,11},{12,13},{... | collective-permute-start | bytes 221192 | tf_op jit(solution)/shard_map/ppermute | solution.py:24
  32.9 6.5 %collective-permute-start.9 = (f32[144,1,128]{2,0,1:T(8,128)S(1)}, f32[144,1,128]{2,0,1:T(8,128)S(1)}, u32[]{:S(2)}, u32[]{:S(2)}) collective-permute-start(f32[144,1,128]{2,0,1:T(8,128)S(1)} %get-tuple-element.146), channel_id=1, source_target_pairs={{1,0},{2,1},{3,2},{5,4},{6,5},{7,6},{9,8},{10,9},{11,10},{13,12},{... | collective-permute-start | bytes 221192 | tf_op jit(solution)/shard_map/ppermute | solution.py:26
  34.9 5.8 %collective-permute-start.6 = (f32[8,8,128]{2,0,1:T(8,128)S(1)}, f32[8,8,128]{2,0,1:T(8,128)S(1)}, u32[]{:S(2)}, u32[]{:S(2)}) collective-permute-start(f32[8,8,128]{2,0,1:T(8,128)S(1)} %get-tuple-element.161), channel_id=1, source_target_pairs={{0,4},{4,8},{8,12},{12,16},{16,20},{20,24},{24,28},{28,0},{1,5},{5... | collective-permute-start | bytes 98312 | tf_op jit(solution)/shard_map/ppermute | solution.py:24
  34.9 5.7 %collective-permute-start.7 = (f32[8,8,128]{2,0,1:T(8,128)S(1)}, f32[8,8,128]{2,0,1:T(8,128)S(1)}, u32[]{:S(2)}, u32[]{:S(2)}) collective-permute-start(f32[8,8,128]{2,0,1:T(8,128)S(1)} %get-tuple-element.162), channel_id=1, source_target_pairs={{4,0},{8,4},{12,8},{16,12},{20,16},{24,20},{28,24},{0,28},{5,1},{9... | collective-permute-start | bytes 98312 | tf_op jit(solution)/shard_map/ppermute | solution.py:26
  41.1 11.2 %copy-start.4 = (f32[144,8,128]{2,0,1:T(8,128)}, f32[144,8,128]{2,0,1:T(8,128)S(1)}, u32[]{:S(2)}) copy-start(f32[144,8,128]{2,0,1:T(8,128)S(1)} %get-tuple-element.114) | copy-start | bytes 1769476
  41.1 6.5 %collective-permute-start.10 = (f32[144,1,128]{2,0,1:T(8,128)S(1)}, f32[144,1,128]{2,0,1:T(8,128)S(1)}, u32[]{:S(2)}, u32[]{:S(2)}) collective-permute-start(f32[144,1,128]{2,0,1:T(8,128)S(1)} %get-tuple-element.143), channel_id=1, source_target_pairs={{0,1},{1,2},{2,3},{4,5},{5,6},{6,7},{8,9},{9,10},{10,11},{12,13},{... | collective-permute-start | bytes 221192 | tf_op jit(solution)/shard_map/ppermute | solution.py:24
  45.6 5.7 %collective-permute-start.11 = (f32[144,1,128]{2,0,1:T(8,128)S(1)}, f32[144,1,128]{2,0,1:T(8,128)S(1)}, u32[]{:S(2)}, u32[]{:S(2)}) collective-permute-start(f32[144,1,128]{2,0,1:T(8,128)S(1)} %get-tuple-element.144), channel_id=1, source_target_pairs={{1,0},{2,1},{3,2},{5,4},{6,5},{7,6},{9,8},{10,9},{11,10},{13,12},{... | collective-permute-start | bytes 221192 | tf_op jit(solution)/shard_map/ppermute | solution.py:26
  53.4 4.3 %collective-permute-start.12 = (f32[144,1,128]{2,0,1:T(8,128)}, f32[144,1,128]{2,0,1:T(8,128)S(1)}, u32[]{:S(2)}, u32[]{:S(2)}) collective-permute-start(f32[144,1,128]{2,0,1:T(8,128)} %get-tuple-element.141), channel_id=1, source_target_pairs={{0,1},{1,2},{2,3},{4,5},{5,6},{6,7},{8,9},{9,10},{10,11},{12,13},{... | collective-permute-start | bytes 221192 | tf_op jit(solution)/shard_map/ppermute | solution.py:24
  55.3 6.0 %collective-permute-start.13 = (f32[144,1,128]{2,0,1:T(8,128)}, f32[144,1,128]{2,0,1:T(8,128)}, u32[]{:S(2)}, u32[]{:S(2)}) collective-permute-start(f32[144,1,128]{2,0,1:T(8,128)} %get-tuple-element.142), channel_id=1, source_target_pairs={{1,0},{2,1},{3,2},{5,4},{6,5},{7,6},{9,8},{10,9},{11,10},{13,12},{... | collective-permute-start | bytes 221192 | tf_op jit(solution)/shard_map/ppermute | solution.py:26
  63.0 1.1 copy-start.5
  64.9 5.9 %collective-permute-start.14 = (f32[8,8,128]{2,0,1:T(8,128)S(1)}, f32[8,8,128]{2,0,1:T(8,128)S(1)}, u32[]{:S(2)}, u32[]{:S(2)}) collective-permute-start(f32[8,8,128]{2,0,1:T(8,128)S(1)} %get-tuple-element.140), channel_id=1, source_target_pairs={{28,0},{0,4},{4,8},{8,12},{12,16},{16,20},{20,24},{24,28},{29,1},{... | collective-permute-start | bytes 98312 | tf_op jit(solution)/shard_map/ppermute | solution.py:36
  65.2 5.6 %collective-permute-start.15 = (f32[8,8,128]{2,0,1:T(8,128)S(1)}, f32[8,8,128]{2,0,1:T(8,128)S(1)}, u32[]{:S(2)}, u32[]{:S(2)}) collective-permute-start(f32[8,8,128]{2,0,1:T(8,128)S(1)} %get-tuple-element.139), channel_id=1, source_target_pairs={{4,0},{8,4},{12,8},{16,12},{20,16},{24,20},{28,24},{0,28},{5,1},{9... | collective-permute-start | bytes 98312 | tf_op jit(solution)/shard_map/ppermute | solution.py:36
  70.8 5.2 %collective-permute-start.17 = (f32[1,8,128]{2,0,1:T(1,128)S(1)}, f32[1,8,128]{2,0,1:T(1,128)S(1)}, u32[]{:S(2)}, u32[]{:S(2)}) collective-permute-start(f32[1,8,128]{2,0,1:T(1,128)S(1)} %slice.1115), channel_id=1, source_target_pairs={{4,0},{8,4},{12,8},{16,12},{20,16},{24,20},{28,24},{0,28},{5,1},{9... | collective-permute-start | bytes 12296 | tf_op jit(solution)/shard_map/ppermute | solution.py:26
  75.3 5.4 %collective-permute-start.16 = (f32[1,8,128]{2,0,1:T(1,128)S(1)}, f32[1,8,128]{2,0,1:T(1,128)S(1)}, u32[]{:S(2)}, u32[]{:S(2)}) collective-permute-start(f32[1,8,128]{2,0,1:T(1,128)S(1)} %slice.1114), channel_id=1, source_target_pairs={{0,4},{4,8},{8,12},{12,16},{16,20},{20,24},{24,28},{28,0},{1,5},{5... | collective-permute-start | bytes 12296 | tf_op jit(solution)/shard_map/ppermute | solution.py:24
  80.7 6.2 %collective-permute-start.18 = (f32[130,1,128]{2,0,1:T(8,128)S(1)}, f32[130,1,128]{2,0,1:T(8,128)S(1)}, u32[]{:S(2)}, u32[]{:S(2)}) collective-permute-start(f32[130,1,128]{2,0,1:T(8,128)S(1)} %get-tuple-element.151), channel_id=1, source_target_pairs={{0,1},{1,2},{2,3},{4,5},{5,6},{6,7},{8,9},{9,10},{10,11},{12,13},{... | collective-permute-start | bytes 199688 | tf_op jit(solution)/shard_map/ppermute | solution.py:24
  84.9 5.6 %collective-permute-start.19 = (f32[130,1,128]{2,0,1:T(8,128)S(1)}, f32[130,1,128]{2,0,1:T(8,128)S(1)}, u32[]{:S(2)}, u32[]{:S(2)}) collective-permute-start(f32[130,1,128]{2,0,1:T(8,128)S(1)} %get-tuple-element.152), channel_id=1, source_target_pairs={{1,0},{2,1},{3,2},{5,4},{6,5},{7,6},{9,8},{10,9},{11,10},{13,12},{... | collective-permute-start | bytes 199688 | tf_op jit(solution)/shard_map/ppermute | solution.py:26
  92.8 5.5 %collective-permute-start.20 = (f32[8,8,128]{2,0,1:T(8,128)S(1)}, f32[8,8,128]{2,0,1:T(8,128)S(1)}, u32[]{:S(2)}, u32[]{:S(2)}) collective-permute-start(f32[8,8,128]{2,0,1:T(8,128)S(1)} %get-tuple-element.159), channel_id=1, source_target_pairs={{0,4},{4,8},{8,12},{12,16},{16,20},{20,24},{24,28},{28,0},{1,5},{5... | collective-permute-start | bytes 98312 | tf_op jit(solution)/shard_map/ppermute | solution.py:24
  92.8 5.5 %collective-permute-start.21 = (f32[8,8,128]{2,0,1:T(8,128)S(1)}, f32[8,8,128]{2,0,1:T(8,128)S(1)}, u32[]{:S(2)}, u32[]{:S(2)}) collective-permute-start(f32[8,8,128]{2,0,1:T(8,128)S(1)} %get-tuple-element.160), channel_id=1, source_target_pairs={{4,0},{8,4},{12,8},{16,12},{20,16},{24,20},{28,24},{0,28},{5,1},{9... | collective-permute-start | bytes 98312 | tf_op jit(solution)/shard_map/ppermute | solution.py:26
  98.4 5.0 %collective-permute-start.22 = (f32[144,1,128]{2,0,1:T(8,128)S(1)}, f32[144,1,128]{2,0,1:T(8,128)S(1)}, u32[]{:S(2)}, u32[]{:S(2)}) collective-permute-start(f32[144,1,128]{2,0,1:T(8,128)S(1)} %get-tuple-element.137), channel_id=1, source_target_pairs={{0,1},{1,2},{2,3},{4,5},{5,6},{6,7},{8,9},{9,10},{10,11},{12,13},{... | collective-permute-start | bytes 221192 | tf_op jit(solution)/shard_map/ppermute | solution.py:24
  101.4 5.7 %collective-permute-start.23 = (f32[144,1,128]{2,0,1:T(8,128)S(1)}, f32[144,1,128]{2,0,1:T(8,128)S(1)}, u32[]{:S(2)}, u32[]{:S(2)}) collective-permute-start(f32[144,1,128]{2,0,1:T(8,128)S(1)} %get-tuple-element.138), channel_id=1, source_target_pairs={{1,0},{2,1},{3,2},{5,4},{6,5},{7,6},{9,8},{10,9},{11,10},{13,12},{... | collective-permute-start | bytes 221192 | tf_op jit(solution)/shard_map/ppermute | solution.py:26
  108.5 8.6 %copy-start.6 = (f32[144,8,128]{2,0,1:T(8,128)}, f32[144,8,128]{2,0,1:T(8,128)S(1)}, u32[]{:S(2)}) copy-start(f32[144,8,128]{2,0,1:T(8,128)S(1)} %get-tuple-element.110) | copy-start | bytes 1769476
  108.5 4.5 %collective-permute-start.24 = (f32[144,1,128]{2,0,1:T(8,128)S(1)}, f32[144,1,128]{2,0,1:T(8,128)S(1)}, u32[]{:S(2)}, u32[]{:S(2)}) collective-permute-start(f32[144,1,128]{2,0,1:T(8,128)S(1)} %get-tuple-element.135), channel_id=1, source_target_pairs={{0,1},{1,2},{2,3},{4,5},{5,6},{6,7},{8,9},{9,10},{10,11},{12,13},{... | collective-permute-start | bytes 221192 | tf_op jit(solution)/shard_map/ppermute | solution.py:24
  110.4 5.7 %collective-permute-start.25 = (f32[144,1,128]{2,0,1:T(8,128)S(1)}, f32[144,1,128]{2,0,1:T(8,128)S(1)}, u32[]{:S(2)}, u32[]{:S(2)}) collective-permute-start(f32[144,1,128]{2,0,1:T(8,128)S(1)} %get-tuple-element.136), channel_id=1, source_target_pairs={{1,0},{2,1},{3,2},{5,4},{6,5},{7,6},{9,8},{10,9},{11,10},{13,12},{... | collective-permute-start | bytes 221192 | tf_op jit(solution)/shard_map/ppermute | solution.py:26
  119.0 4.3 %collective-permute-start.26 = (f32[144,1,128]{2,0,1:T(8,128)}, f32[144,1,128]{2,0,1:T(8,128)S(1)}, u32[]{:S(2)}, u32[]{:S(2)}) collective-permute-start(f32[144,1,128]{2,0,1:T(8,128)} %get-tuple-element.133), channel_id=1, source_target_pairs={{0,1},{1,2},{2,3},{4,5},{5,6},{6,7},{8,9},{9,10},{10,11},{12,13},{... | collective-permute-start | bytes 221192 | tf_op jit(solution)/shard_map/ppermute | solution.py:24
  120.9 5.9 %collective-permute-start.27 = (f32[144,1,128]{2,0,1:T(8,128)}, f32[144,1,128]{2,0,1:T(8,128)S(1)}, u32[]{:S(2)}, u32[]{:S(2)}) collective-permute-start(f32[144,1,128]{2,0,1:T(8,128)} %get-tuple-element.134), channel_id=1, source_target_pairs={{1,0},{2,1},{3,2},{5,4},{6,5},{7,6},{9,8},{10,9},{11,10},{13,12},{... | collective-permute-start | bytes 221192 | tf_op jit(solution)/shard_map/ppermute | solution.py:26
  128.7 1.1 copy-start.7
  130.6 5.8 %collective-permute-start.28 = (f32[8,8,128]{2,0,1:T(8,128)S(1)}, f32[8,8,128]{2,0,1:T(8,128)S(1)}, u32[]{:S(2)}, u32[]{:S(2)}) collective-permute-start(f32[8,8,128]{2,0,1:T(8,128)S(1)} %get-tuple-element.132), channel_id=1, source_target_pairs={{28,0},{0,4},{4,8},{8,12},{12,16},{16,20},{20,24},{24,28},{29,1},{... | collective-permute-start | bytes 98312 | tf_op jit(solution)/shard_map/ppermute | solution.py:36
  130.7 5.7 %collective-permute-start.29 = (f32[8,8,128]{2,0,1:T(8,128)S(1)}, f32[8,8,128]{2,0,1:T(8,128)S(1)}, u32[]{:S(2)}, u32[]{:S(2)}) collective-permute-start(f32[8,8,128]{2,0,1:T(8,128)S(1)} %get-tuple-element.131), channel_id=1, source_target_pairs={{4,0},{8,4},{12,8},{16,12},{20,16},{24,20},{28,24},{0,28},{5,1},{9... | collective-permute-start | bytes 98312 | tf_op jit(solution)/shard_map/ppermute | solution.py:36
  136.4 5.1 %collective-permute-start.31 = (f32[1,8,128]{2,0,1:T(1,128)S(1)}, f32[1,8,128]{2,0,1:T(1,128)S(1)}, u32[]{:S(2)}, u32[]{:S(2)}) collective-permute-start(f32[1,8,128]{2,0,1:T(1,128)S(1)} %slice.1166), channel_id=1, source_target_pairs={{4,0},{8,4},{12,8},{16,12},{20,16},{24,20},{28,24},{0,28},{5,1},{9... | collective-permute-start | bytes 12296 | tf_op jit(solution)/shard_map/ppermute | solution.py:26
  140.8 5.3 %collective-permute-start.30 = (f32[1,8,128]{2,0,1:T(1,128)S(1)}, f32[1,8,128]{2,0,1:T(1,128)S(1)}, u32[]{:S(2)}, u32[]{:S(2)}) collective-permute-start(f32[1,8,128]{2,0,1:T(1,128)S(1)} %slice.1165), channel_id=1, source_target_pairs={{0,4},{4,8},{8,12},{12,16},{16,20},{20,24},{24,28},{28,0},{1,5},{5... | collective-permute-start | bytes 12296 | tf_op jit(solution)/shard_map/ppermute | solution.py:24
  146.1 6.3 %collective-permute-start.32 = (f32[130,1,128]{2,0,1:T(8,128)S(1)}, f32[130,1,128]{2,0,1:T(8,128)S(1)}, u32[]{:S(2)}, u32[]{:S(2)}) collective-permute-start(f32[130,1,128]{2,0,1:T(8,128)S(1)} %get-tuple-element.149), channel_id=1, source_target_pairs={{0,1},{1,2},{2,3},{4,5},{5,6},{6,7},{8,9},{9,10},{10,11},{12,13},{... | collective-permute-start | bytes 199688 | tf_op jit(solution)/shard_map/ppermute | solution.py:24
  150.5 5.6 %collective-permute-start.33 = (f32[130,1,128]{2,0,1:T(8,128)S(1)}, f32[130,1,128]{2,0,1:T(8,128)S(1)}, u32[]{:S(2)}, u32[]{:S(2)}) collective-permute-start(f32[130,1,128]{2,0,1:T(8,128)S(1)} %get-tuple-element.150), channel_id=1, source_target_pairs={{1,0},{2,1},{3,2},{5,4},{6,5},{7,6},{9,8},{10,9},{11,10},{13,12},{... | collective-permute-start | bytes 199688 | tf_op jit(solution)/shard_map/ppermute | solution.py:26
  158.3 5.5 %collective-permute-start.34 = (f32[8,8,128]{2,0,1:T(8,128)S(1)}, f32[8,8,128]{2,0,1:T(8,128)S(1)}, u32[]{:S(2)}, u32[]{:S(2)}) collective-permute-start(f32[8,8,128]{2,0,1:T(8,128)S(1)} %get-tuple-element.157), channel_id=1, source_target_pairs={{0,4},{4,8},{8,12},{12,16},{16,20},{20,24},{24,28},{28,0},{1,5},{5... | collective-permute-start | bytes 98312 | tf_op jit(solution)/shard_map/ppermute | solution.py:24
  158.4 5.5 %collective-permute-start.35 = (f32[8,8,128]{2,0,1:T(8,128)S(1)}, f32[8,8,128]{2,0,1:T(8,128)S(1)}, u32[]{:S(2)}, u32[]{:S(2)}) collective-permute-start(f32[8,8,128]{2,0,1:T(8,128)S(1)} %get-tuple-element.158), channel_id=1, source_target_pairs={{4,0},{8,4},{12,8},{16,12},{20,16},{24,20},{28,24},{0,28},{5,1},{9... | collective-permute-start | bytes 98312 | tf_op jit(solution)/shard_map/ppermute | solution.py:26
  163.9 5.0 %collective-permute-start.36 = (f32[144,1,128]{2,0,1:T(8,128)S(1)}, f32[144,1,128]{2,0,1:T(8,128)S(1)}, u32[]{:S(2)}, u32[]{:S(2)}) collective-permute-start(f32[144,1,128]{2,0,1:T(8,128)S(1)} %get-tuple-element.129), channel_id=1, source_target_pairs={{0,1},{1,2},{2,3},{4,5},{5,6},{6,7},{8,9},{9,10},{10,11},{12,13},{... | collective-permute-start | bytes 221192 | tf_op jit(solution)/shard_map/ppermute | solution.py:24
  166.9 5.7 %collective-permute-start.37 = (f32[144,1,128]{2,0,1:T(8,128)S(1)}, f32[144,1,128]{2,0,1:T(8,128)S(1)}, u32[]{:S(2)}, u32[]{:S(2)}) collective-permute-start(f32[144,1,128]{2,0,1:T(8,128)S(1)} %get-tuple-element.130), channel_id=1, source_target_pairs={{1,0},{2,1},{3,2},{5,4},{6,5},{7,6},{9,8},{10,9},{11,10},{13,12},{... | collective-permute-start | bytes 221192 | tf_op jit(solution)/shard_map/ppermute | solution.py:26
  174.0 4.3 %collective-permute-start.38 = (f32[144,1,128]{2,0,1:T(8,128)S(1)}, f32[144,1,128]{2,0,1:T(8,128)S(1)}, u32[]{:S(2)}, u32[]{:S(2)}) collective-permute-start(f32[144,1,128]{2,0,1:T(8,128)S(1)} %get-tuple-element.127), channel_id=1, source_target_pairs={{0,1},{1,2},{2,3},{4,5},{5,6},{6,7},{8,9},{9,10},{10,11},{12,13},{... | collective-permute-start | bytes 221192 | tf_op jit(solution)/shard_map/ppermute | solution.py:24
  175.9 5.7 %collective-permute-start.39 = (f32[144,1,128]{2,0,1:T(8,128)S(1)}, f32[144,1,128]{2,0,1:T(8,128)S(1)}, u32[]{:S(2)}, u32[]{:S(2)}) collective-permute-start(f32[144,1,128]{2,0,1:T(8,128)S(1)} %get-tuple-element.128), channel_id=1, source_target_pairs={{1,0},{2,1},{3,2},{5,4},{6,5},{7,6},{9,8},{10,9},{11,10},{13,12},{... | collective-permute-start | bytes 221192 | tf_op jit(solution)/shard_map/ppermute | solution.py:26
  183.0 4.3 %collective-permute-start.40 = (f32[144,1,128]{2,0,1:T(8,128)S(1)}, f32[144,1,128]{2,0,1:T(8,128)S(1)}, u32[]{:S(2)}, u32[]{:S(2)}) collective-permute-start(f32[144,1,128]{2,0,1:T(8,128)S(1)} %get-tuple-element.125), channel_id=1, source_target_pairs={{0,1},{1,2},{2,3},{4,5},{5,6},{6,7},{8,9},{9,10},{10,11},{12,13},{... | collective-permute-start | bytes 221192 | tf_op jit(solution)/shard_map/ppermute | solution.py:24
  184.9 5.7 %collective-permute-start.41 = (f32[144,1,128]{2,0,1:T(8,128)S(1)}, f32[144,1,128]{2,0,1:T(8,128)S(1)}, u32[]{:S(2)}, u32[]{:S(2)}) collective-permute-start(f32[144,1,128]{2,0,1:T(8,128)S(1)} %get-tuple-element.126), channel_id=1, source_target_pairs={{1,0},{2,1},{3,2},{5,4},{6,5},{7,6},{9,8},{10,9},{11,10},{13,12},{... | collective-permute-start | bytes 221192 | tf_op jit(solution)/shard_map/ppermute | solution.py:26
  192.4 5.8 %collective-permute-start.42 = (f32[8,8,128]{2,0,1:T(8,128)S(1)}, f32[8,8,128]{2,0,1:T(8,128)S(1)}, u32[]{:S(2)}, u32[]{:S(2)}) collective-permute-start(f32[8,8,128]{2,0,1:T(8,128)S(1)} %get-tuple-element.124), channel_id=1, source_target_pairs={{28,0},{0,4},{4,8},{8,12},{12,16},{16,20},{20,24},{24,28},{29,1},{... | collective-permute-start | bytes 98312 | tf_op jit(solution)/shard_map/ppermute | solution.py:36
  192.6 5.7 %collective-permute-start.43 = (f32[8,8,128]{2,0,1:T(8,128)S(1)}, f32[8,8,128]{2,0,1:T(8,128)S(1)}, u32[]{:S(2)}, u32[]{:S(2)}) collective-permute-start(f32[8,8,128]{2,0,1:T(8,128)S(1)} %get-tuple-element.123), channel_id=1, source_target_pairs={{4,0},{8,4},{12,8},{16,12},{20,16},{24,20},{28,24},{0,28},{5,1},{9... | collective-permute-start | bytes 98312 | tf_op jit(solution)/shard_map/ppermute | solution.py:36
  198.3 5.1 %collective-permute-start.45 = (f32[1,8,128]{2,0,1:T(1,128)S(1)}, f32[1,8,128]{2,0,1:T(1,128)S(1)}, u32[]{:S(2)}, u32[]{:S(2)}) collective-permute-start(f32[1,8,128]{2,0,1:T(1,128)S(1)} %slice.1217), channel_id=1, source_target_pairs={{4,0},{8,4},{12,8},{16,12},{20,16},{24,20},{28,24},{0,28},{5,1},{9... | collective-permute-start | bytes 12296 | tf_op jit(solution)/shard_map/ppermute | solution.py:26
  202.6 5.3 %collective-permute-start.44 = (f32[1,8,128]{2,0,1:T(1,128)S(1)}, f32[1,8,128]{2,0,1:T(1,128)S(1)}, u32[]{:S(2)}, u32[]{:S(2)}) collective-permute-start(f32[1,8,128]{2,0,1:T(1,128)S(1)} %slice.1216), channel_id=1, source_target_pairs={{0,4},{4,8},{8,12},{12,16},{16,20},{20,24},{24,28},{28,0},{1,5},{5... | collective-permute-start | bytes 12296 | tf_op jit(solution)/shard_map/ppermute | solution.py:24
  208.0 6.4 %collective-permute-start.46 = (f32[130,1,128]{2,0,1:T(8,128)S(1)}, f32[130,1,128]{2,0,1:T(8,128)S(1)}, u32[]{:S(2)}, u32[]{:S(2)}) collective-permute-start(f32[130,1,128]{2,0,1:T(8,128)S(1)} %get-tuple-element.147), channel_id=1, source_target_pairs={{0,1},{1,2},{2,3},{4,5},{5,6},{6,7},{8,9},{9,10},{10,11},{12,13},{... | collective-permute-start | bytes 199688 | tf_op jit(solution)/shard_map/ppermute | solution.py:24
  212.2 5.6 %collective-permute-start.47 = (f32[130,1,128]{2,0,1:T(8,128)S(1)}, f32[130,1,128]{2,0,1:T(8,128)S(1)}, u32[]{:S(2)}, u32[]{:S(2)}) collective-permute-start(f32[130,1,128]{2,0,1:T(8,128)S(1)} %get-tuple-element.148), channel_id=1, source_target_pairs={{1,0},{2,1},{3,2},{5,4},{6,5},{7,6},{9,8},{10,9},{11,10},{13,12},{... | collective-permute-start | bytes 199688 | tf_op jit(solution)/shard_map/ppermute | solution.py:26
  219.2 5.5 %collective-permute-start.48 = (f32[8,8,128]{2,0,1:T(8,128)S(1)}, f32[8,8,128]{2,0,1:T(8,128)S(1)}, u32[]{:S(2)}, u32[]{:S(2)}) collective-permute-start(f32[8,8,128]{2,0,1:T(8,128)S(1)} %get-tuple-element.155), channel_id=1, source_target_pairs={{0,4},{4,8},{8,12},{12,16},{16,20},{20,24},{24,28},{28,0},{1,5},{5... | collective-permute-start | bytes 98312 | tf_op jit(solution)/shard_map/ppermute | solution.py:24
  219.2 5.5 %collective-permute-start.49 = (f32[8,8,128]{2,0,1:T(8,128)S(1)}, f32[8,8,128]{2,0,1:T(8,128)S(1)}, u32[]{:S(2)}, u32[]{:S(2)}) collective-permute-start(f32[8,8,128]{2,0,1:T(8,128)S(1)} %get-tuple-element.156), channel_id=1, source_target_pairs={{4,0},{8,4},{12,8},{16,12},{20,16},{24,20},{28,24},{0,28},{5,1},{9... | collective-permute-start | bytes 98312 | tf_op jit(solution)/shard_map/ppermute | solution.py:26
  224.8 5.0 %collective-permute-start.50 = (f32[144,1,128]{2,0,1:T(8,128)S(1)}, f32[144,1,128]{2,0,1:T(8,128)S(1)}, u32[]{:S(2)}, u32[]{:S(2)}) collective-permute-start(f32[144,1,128]{2,0,1:T(8,128)S(1)} %get-tuple-element.121), channel_id=1, source_target_pairs={{0,1},{1,2},{2,3},{4,5},{5,6},{6,7},{8,9},{9,10},{10,11},{12,13},{... | collective-permute-start | bytes 221192 | tf_op jit(solution)/shard_map/ppermute | solution.py:24
  227.8 5.7 %collective-permute-start.51 = (f32[144,1,128]{2,0,1:T(8,128)S(1)}, f32[144,1,128]{2,0,1:T(8,128)S(1)}, u32[]{:S(2)}, u32[]{:S(2)}) collective-permute-start(f32[144,1,128]{2,0,1:T(8,128)S(1)} %get-tuple-element.122), channel_id=1, source_target_pairs={{1,0},{2,1},{3,2},{5,4},{6,5},{7,6},{9,8},{10,9},{11,10},{13,12},{... | collective-permute-start | bytes 221192 | tf_op jit(solution)/shard_map/ppermute | solution.py:26
  234.8 4.3 %collective-permute-start.52 = (f32[144,1,128]{2,0,1:T(8,128)S(1)}, f32[144,1,128]{2,0,1:T(8,128)S(1)}, u32[]{:S(2)}, u32[]{:S(2)}) collective-permute-start(f32[144,1,128]{2,0,1:T(8,128)S(1)} %get-tuple-element.119), channel_id=1, source_target_pairs={{0,1},{1,2},{2,3},{4,5},{5,6},{6,7},{8,9},{9,10},{10,11},{12,13},{... | collective-permute-start | bytes 221192 | tf_op jit(solution)/shard_map/ppermute | solution.py:24
  236.8 5.7 %collective-permute-start.53 = (f32[144,1,128]{2,0,1:T(8,128)S(1)}, f32[144,1,128]{2,0,1:T(8,128)S(1)}, u32[]{:S(2)}, u32[]{:S(2)}) collective-permute-start(f32[144,1,128]{2,0,1:T(8,128)S(1)} %get-tuple-element.120), channel_id=1, source_target_pairs={{1,0},{2,1},{3,2},{5,4},{6,5},{7,6},{9,8},{10,9},{11,10},{13,12},{... | collective-permute-start | bytes 221192 | tf_op jit(solution)/shard_map/ppermute | solution.py:26
  243.9 4.3 %collective-permute-start.54 = (f32[144,1,128]{2,0,1:T(8,128)S(1)}, f32[144,1,128]{2,0,1:T(8,128)S(1)}, u32[]{:S(2)}, u32[]{:S(2)}) collective-permute-start(f32[144,1,128]{2,0,1:T(8,128)S(1)} %get-tuple-element.117), channel_id=1, source_target_pairs={{0,1},{1,2},{2,3},{4,5},{5,6},{6,7},{8,9},{9,10},{10,11},{12,13},{... | collective-permute-start | bytes 221192 | tf_op jit(solution)/shard_map/ppermute | solution.py:24
  245.8 5.7 %collective-permute-start.55 = (f32[144,1,128]{2,0,1:T(8,128)S(1)}, f32[144,1,128]{2,0,1:T(8,128)S(1)}, u32[]{:S(2)}, u32[]{:S(2)}) collective-permute-start(f32[144,1,128]{2,0,1:T(8,128)S(1)} %get-tuple-element.118), channel_id=1, source_target_pairs={{1,0},{2,1},{3,2},{5,4},{6,5},{7,6},{9,8},{10,9},{11,10},{13,12},{... | collective-permute-start | bytes 221192 | tf_op jit(solution)/shard_map/ppermute | solution.py:26
  253.3 5.8 %collective-permute-start.56 = (f32[8,8,128]{2,0,1:T(8,128)S(1)}, f32[8,8,128]{2,0,1:T(8,128)S(1)}, u32[]{:S(2)}, u32[]{:S(2)}) collective-permute-start(f32[8,8,128]{2,0,1:T(8,128)S(1)} %get-tuple-element.116), channel_id=1, source_target_pairs={{28,0},{0,4},{4,8},{8,12},{12,16},{16,20},{20,24},{24,28},{29,1},{... | collective-permute-start | bytes 98312 | tf_op jit(solution)/shard_map/ppermute | solution.py:36
  253.4 5.7 %collective-permute-start.57 = (f32[8,8,128]{2,0,1:T(8,128)S(1)}, f32[8,8,128]{2,0,1:T(8,128)S(1)}, u32[]{:S(2)}, u32[]{:S(2)}) collective-permute-start(f32[8,8,128]{2,0,1:T(8,128)S(1)} %get-tuple-element.115), channel_id=1, source_target_pairs={{4,0},{8,4},{12,8},{16,12},{20,16},{24,20},{28,24},{0,28},{5,1},{9... | collective-permute-start | bytes 98312 | tf_op jit(solution)/shard_map/ppermute | solution.py:36
  (5 other events, 5.0 us)
where the time goes:
time: 262 us; the launch traced here: 260 us
  starting transfers between devices  140 us (53%)
  waiting for transfers between devices  82.6 us (32%)
  other arithmetic  25.5 us (10%)
  local copies, waits for them, and re-layouts  10.3 us (4%)
    ppermute x25, starting transfers between devices, extended(): lax.ppermute(head, axis, [((i + 1) % count, i) for i in range(ends)])  73.8 us
    ppermute x25, waiting for transfers between devices, extended(): lax.ppermute(head, axis, [((i + 1) % count, i) for i in range(ends)])  54.8 us
    ppermute x25, starting transfers between devices, extended(): lax.ppermute(tail, axis, [(i, (i + 1) % count) for i in range(ends)])  48.3 us
    ppermute x25, waiting for transfers between devices, extended(): lax.ppermute(tail, axis, [(i, (i + 1) % count) for i in range(ends)])  23.2 us
    ppermute x8, starting transfers between devices, passed_along(): return lax.ppermute(block, axis, route)  18.3 us
    concatenate x16, other arithmetic, extended(): jnp.concatenate([lax.ppermute(tail, axis, [(i, (i + 1) % count) for i in...  9.47 us
    unnamed x23, local copies, waits for them, and re-layouts  7 us
    add x16, other arithmetic, smooth(): along_x = 0.5 * (padded[:-2] + padded[2:]) + padded[1:-1]  5.24 us
  transfers between devices with their start and end apart: 58, of which 31 were waited for; matrix products, arithmetic and copies ran while one was open for 1% of the time, Pallas kernels for 0%

commit v1 on v0

v1 whole, which is shorter than its diff:
```python
import jax
import jax.numpy as jnp
from jax import lax
from jax.experimental import pallas as pl
from jax.experimental.pallas import tpu as pltpu
from jax.sharding import PartitionSpec as P

OV = 8
PASSES = 3
SWEEPS = 2
HALO = PASSES + 1
UNROLL = 4
MESH = pl.DeviceIdType.MESH

low_end = 0.05
high_end = 2.2
centre_weight = 1.0 + 1.0 / 7.0

DIRECTIONS = [(0, 1), (0, -1), (1, 0), (-1, 0), (1, 1), (1, -1), (-1, 1), (-1, -1)]


def cheby_terms(passes):
    centre = (high_end + low_end) / 2.0
    half_width = (high_end - low_end) / 2.0
    sigma_value = centre / half_width
    ratio_now = 1.0 / sigma_value
    terms = []
    for repeat in range(passes):
        ratio_next = 1.0 / (2.0 * sigma_value - ratio_now)
        terms.append((ratio_next * ratio_now, 2.0 * ratio_next / half_width))
        ratio_now = ratio_next
    return centre, terms


def kernel(
    source, shift, start, out,
    F, S, C, R0, R1, R2, D1, D2, X, Y,
    own_sem, out_sem, init_send, init_recv, x_send, x_recv, f_send, f_recv,
    y_send, y_recv, last_send, last_recv,
):
    n, ny, nz = source.shape
    blocks, bands = lax.axis_size("blk"), lax.axis_size("narrow")
    b, w = lax.axis_index("blk"), lax.axis_index("narrow")
    base = OV + 1
    edge = 2 * OV + 1
    has_low, has_high = w > 0, w < bands - 1
    inv_c = 1.0 / cheby_terms(PASSES)[0]
    terms = cheby_terms(PASSES)[1]

    def device(dx, dy):
        return (lax.rem(b + dx + blocks, blocks), w + dy)

    def when_to(dy, act):
        if dy == 0:
            act()
        else:
            pl.when(has_high if dy > 0 else has_low)(act)

    def when_from(dy, act):
        when_to(-dy, act)

    zero_rows = jnp.zeros((2 * HALO + ny, nz), jnp.float32)

    def clear(refs, first, last):
        def body(i, carry):
            for ref in refs:
                ref[i] = zero_rows
            return carry
        lax.fori_loop(first, last, body, 0)

    clear((R0, D1, D2), 0, n + 2 * base)

    @pl.when(jnp.logical_or(w == 0, w == bands - 1))
    def _():
        clear((F, S, C), 0, n + 2 * base)

        def body_x(i, carry):
            for k in range(X.shape[0]):
                X[k, i] = zero_rows
            return carry

        lax.fori_loop(0, edge, body_x, 0)

        def body_y(i, carry):
            for k in range(Y.shape[0]):
                Y[k, i] = jnp.zeros((2 * HALO, nz), jnp.float32)
            return carry
        lax.fori_loop(0, Y.shape[1], body_y, 0)

    own = [
        pltpu.make_async_copy(
            array, buf.at[pl.ds(base, n), pl.ds(HALO, ny)], own_sem.at[k])
        for k, (array, buf) in enumerate(((start, F), (source, S), (shift, C)))
    ]
    for copy in own:
        copy.start()

    barrier = pltpu.get_barrier_semaphore()
    for dx, dy in DIRECTIONS:
        def greet(dx=dx, dy=dy):
            pl.semaphore_signal(barrier, inc=1, device_id=device(dx, dy), device_id_type=MESH)
        when_to(dy, greet)
    pl.semaphore_wait(barrier, 2 + 3 * jnp.where(has_low, 1, 0) + 3 * jnp.where(has_high, 1, 0))

    def rows_of(dy, depth):
        if dy == 0:
            return pl.ds(0, ny), pl.ds(HALO, ny)
        if dy > 0:
            return pl.ds(ny - depth, depth), pl.ds(HALO - depth, depth)
        return pl.ds(0, depth), pl.ds(HALO + ny, depth)

    def layers_of(dx, width):
        if dx == 0:
            return pl.ds(0, n), pl.ds(base, n)
        if dx > 0:
            return pl.ds(n - width, width), pl.ds(base - width, width)
        return pl.ds(0, width), pl.ds(base + n, width)

    def initial(array_index, k):
        dx, dy = DIRECTIONS[k]
        array, buf = ((start, F), (source, S), (shift, C))[array_index]
        wide, deep = (OV + 1, HALO) if array_index == 0 else (OV, HALO - 1)
        from_rows, to_rows = rows_of(dy, deep)
        from_layers, to_layers = layers_of(dx, wide)
        return pltpu.make_async_remote_copy(
            src_ref=array.at[from_layers, from_rows],
            dst_ref=buf.at[to_layers, to_rows],
            send_sem=init_send.at[array_index, k],
            recv_sem=init_recv.at[array_index, k],
            device_id=device(dx, dy), device_id_type=MESH)

    even = lax.rem(b, 2) == 0
    odd = lax.rem(b, 2) == 1

    def all_initial(dirs, field_margin, start_it, send_wait=False):
        for array_index in range(3):
            for k in dirs:
                dx, dy = DIRECTIONS[k]
                if array_index == 0 and dx != 0 and not field_margin:
                    continue
                copy = initial(array_index, k)
                if start_it:
                    when_to(dy, copy.start)
                elif send_wait:
                    when_to(dy, copy.wait_send)
                else:
                    when_from(dy, copy.wait_recv)

    side_dirs, cross_dirs = (0, 1), (2, 3, 4, 5, 6, 7)

    lane = lax.broadcasted_iota(jnp.int32, (8, nz), 1)
    first_lane, last_lane = lane == 0, lane == nz - 1
    row = lax.broadcasted_iota(jnp.int32, (8, nz), 0)

    def weight(top):
        place = w * ny - HALO + top + row
        inside = jnp.logical_and(place >= 0, place < bands * ny)
        return jnp.where(inside, jnp.float32(1.0 / 56.0), jnp.float32(0.0))

    def filter_rows(ref, x, top):
        mid = ref[x, pl.ds(top, 8)]
        return (ref[x, pl.ds(top - 1, 8)] + ref[x, pl.ds(top + 1, 8)]) + (mid + mid)

    def stencil(ref, first, last, tops, emit):
        carry = []
        for top in tops:
            below, here = filter_rows(ref, first - 1, top), filter_rows(ref, first, top)
            carry += [below + here, here]

        def layer(x, carry):
            carry = list(carry)
            for t, top in enumerate(tops):
                pair, here = carry[2 * t], carry[2 * t + 1]
                above = filter_rows(ref, x + 1, top)
                next_pair = here + above
                both = pair + next_pair
                left = jnp.where(first_lane, 0.0, pltpu.roll(both, 1, 1))
                right = jnp.where(last_lane, 0.0, pltpu.roll(both, nz - 1, 1))
                emit(x, top, t, (both + both) + (left + right))
                carry[2 * t], carry[2 * t + 1] = next_pair, above
            return tuple(carry)

        whole = (last - first) // UNROLL

        def body(i, carry):
            for u in range(UNROLL):
                carry = layer(first + i * UNROLL + u, carry)
            return carry

        carry = lax.fori_loop(0, whole, body, tuple(carry))
        for x in range(first + whole * UNROLL, last):
            carry = layer(x, carry)

    wide_tops, own_tops = (1, 2 * HALO + ny - 9), (HALO,)
    wide_weights, own_weights = [weight(t) for t in wide_tops], [weight(t) for t in own_tops]

    def residual(first, last):
        def emit(x, top, t, filtered):
            here = pl.ds(top, 8)
            R0[x, here] = (S[x, here] - (centre_weight + C[x, here]) * F[x, here]) + wide_weights[t] * filtered
        stencil(F, first, last, wide_tops, emit)

    def pass_one(first, last):
        p, q = terms[0]
        def emit(x, top, t, filtered):
            here = pl.ds(top, 8)
            r = R0[x, here]
            image = (centre_weight + C[x, here]) * r - wide_weights[t] * filtered
            r1 = r - inv_c * image
            R1[x, here] = r1
            D1[x, here] = (p * inv_c) * r + q * r1
        stencil(R0, first, last, wide_tops, emit)

    def pass_two(first, last):
        p, q = terms[1]
        def emit(x, top, t, filtered):
            here = pl.ds(top, 8)
            d = D1[x, here]
            r2 = R1[x, here] - ((centre_weight + C[x, here]) * d - wide_weights[t] * filtered)
            R2[x, here] = r2
            D2[x, here] = p * d + q * r2
        stencil(D1, first, last, wide_tops, emit)

    def pass_three(first, last):
        p, q = terms[2]
        def emit(x, top, t, filtered):
            here = pl.ds(top, 8)
            d = D2[x, here]
            r3 = R2[x, here] - ((centre_weight + C[x, here]) * d - own_weights[t] * filtered)
            update = (inv_c * R0[x, here] + D1[x, here]) + (d + (p * d + q * r3))
            F[x, here] = F[x, here] + update
        stencil(D2, first, last, own_tops, emit)

    end = n + 2 * base - 1
    inner = 2 * OV + 2
    outer = end + 1 - inner

    def solve_inside():
        residual(inner, outer)
        pass_one(inner + 1, outer - 1)
        pass_two(inner + 2, outer - 2)
        pass_three(inner + 3, outer - 3)

    def solve_edges():
        for k, run in enumerate((residual, pass_one, pass_two, pass_three)):
            run(1, inner + k)
            run(outer - k, end)

    def across(e, side):
        dx = 1 if side == 0 else -1
        begin = base + n - OV - 1 if dx > 0 else 1
        return pltpu.make_async_remote_copy(
            src_ref=F.at[pl.ds(begin, edge), pl.ds(HALO, ny)],
            dst_ref=X.at[2 * e + side, :, pl.ds(HALO, ny)],
            send_sem=x_send.at[e, side], recv_sem=x_recv.at[e, side],
            device_id=device(dx, 0), device_id_type=MESH)

    def forward(e, side, dy):
        from_row = HALO + ny - HALO if dy > 0 else HALO
        to_row = 0 if dy > 0 else HALO + ny
        k = 2 * side + (0 if dy > 0 else 1)
        return pltpu.make_async_remote_copy(
            src_ref=X.at[2 * e + side, :, pl.ds(from_row, HALO)],
            dst_ref=X.at[2 * e + side, :, pl.ds(to_row, HALO)],
            send_sem=f_send.at[e, k], recv_sem=f_recv.at[e, k],
            device_id=device(0, dy), device_id_type=MESH)

    keep = n - 2 * OV

    def along(e, dy):
        from_row = HALO + ny - HALO if dy > 0 else HALO
        to_row = 0 if dy > 0 else HALO
        k = 0 if dy > 0 else 1
        return pltpu.make_async_remote_copy(
            src_ref=F.at[pl.ds(base + OV, keep), pl.ds(from_row, HALO)],
            dst_ref=Y.at[e, :, pl.ds(to_row, HALO)],
            send_sem=y_send.at[e, k], recv_sem=y_recv.at[e, k],
            device_id=device(0, dy), device_id_type=MESH)

    def last_copy(side):
        dx = 1 if side == 0 else -1
        begin = base + n if dx > 0 else base - OV
        return pltpu.make_async_remote_copy(
            src_ref=F.at[pl.ds(begin, OV), pl.ds(HALO, ny)],
            dst_ref=X.at[side + 2 * (2 * SWEEPS - 1), pl.ds(0, OV), pl.ds(HALO, ny)],
            send_sem=last_send.at[side], recv_sem=last_recv.at[side],
            device_id=device(dx, 0), device_id_type=MESH)

    def send_after(e):
        for side in (0, 1):
            across(e, side).start()
        if e < 2 * SWEEPS - 2:
            for dy in (1, -1):
                when_to(dy, along(e, dy).start)

    def finish_sends(e):
        for side in (0, 1):
            across(e, side).wait_send()
        if e < 2 * SWEEPS - 2:
            for dy in (1, -1):
                when_to(dy, along(e, dy).wait_send)

    def take_halo(e):
        for dy in (1, -1):
            when_from(dy, along(e, dy).wait_recv)

        def body(i, carry):
            F[base + OV + i, pl.ds(0, HALO)] = Y[e, i, pl.ds(0, HALO)]
            F[base + OV + i, pl.ds(HALO + ny, HALO)] = Y[e, i, pl.ds(HALO, HALO)]
            return carry
        lax.fori_loop(0, keep, body, 0)

    def take_margins(e):
        for side in (0, 1):
            across(e, side).wait_recv()
            for dy in (1, -1):
                when_to(dy, forward(e, side, dy).start)
        for side in (0, 1):
            for dy in (1, -1):
                when_from(dy, forward(e, side, dy).wait_recv)

        def body(i, carry):
            F[i] = X[2 * e, i]
            F[base + n - OV + i] = X[2 * e + 1, i]
            return carry
        lax.fori_loop(0, edge, body, 0)
        for side in (0, 1):
            for dy in (1, -1):
                when_to(dy, forward(e, side, dy).wait_send)

    def write_out(first, count, k):
        return pltpu.make_async_copy(
            F.at[pl.ds(base + first, count), pl.ds(HALO, ny)],
            out.at[pl.ds(first, count)], out_sem.at[k])

    all_initial(side_dirs, True, True)

    @pl.when(even)
    def _():
        all_initial(cross_dirs, False, True)
        for copy in own:
            copy.wait()
        all_initial(side_dirs, True, False)
        solve_inside()
        all_initial(cross_dirs, True, False)
        solve_edges()
        send_after(0)
        all_initial(side_dirs, True, False, True)
        all_initial(cross_dirs, False, False, True)
        for sweep in range(1, SWEEPS):
            e = 2 * sweep
            finish_sends(e - 2)
            take_halo(e - 2)
            solve_inside()
            take_margins(e - 1)
            solve_edges()
            send_after(e)
        finish_sends(2 * SWEEPS - 2)
        middle = write_out(OV, n - 2 * OV, 0)
        middle.start()
        for side in (0, 1):
            last_copy(side).wait_recv()

        def body(i, carry):
            here = pl.ds(HALO, ny)
            F[base + i, here] = X[2 * (2 * SWEEPS - 1), i, here]
            F[base + n - OV + i, here] = X[2 * (2 * SWEEPS - 1) + 1, i, here]
            return carry
        lax.fori_loop(0, OV, body, 0)
        low, high = write_out(0, OV, 1), write_out(n - OV, OV, 2)
        low.start()
        high.start()
        middle.wait()
        low.wait()
        high.wait()

    @pl.when(odd)
    def _():
        all_initial(cross_dirs, True, True)
        for copy in own:
            copy.wait()
        all_initial(side_dirs, True, False)
        solve_inside()
        all_initial(cross_dirs, False, False)
        all_initial(side_dirs, True, False, True)
        all_initial(cross_dirs, True, False, True)
        for sweep in range(SWEEPS):
            e = 2 * sweep + 1
            if sweep > 0:
                finish_sends(e - 2)
                take_halo(e - 2)
                solve_inside()
            take_margins(e - 1)
            solve_edges()
            if sweep < SWEEPS - 1:
                send_after(e)
        for side in (0, 1):
            last_copy(side).start()
        whole = write_out(0, n, 0)
        whole.start()
        for side in (0, 1):
            last_copy(side).wait_send()
        whole.wait()


def per_device(source, shift, start_field):
    n, ny, nz = source.shape
    layers, rows = n + 2 * OV + 2, ny + 2 * HALO
    work = pltpu.VMEM((layers, rows, nz), jnp.float32)
    dma = pltpu.SemaphoreType.DMA
    phases = 2 * SWEEPS
    return pl.pallas_call(
        kernel,
        out_shape=jax.ShapeDtypeStruct(source.shape, source.dtype),
        in_specs=[pl.BlockSpec(memory_space=pl.ANY)] * 3,
        out_specs=pl.BlockSpec(memory_space=pl.ANY),
        scratch_shapes=[work] * 8 + [
            pltpu.VMEM((2 * phases, 2 * OV + 1, rows, nz), jnp.float32),
            pltpu.VMEM((phases - 2, n - 2 * OV, 2 * HALO, nz), jnp.float32),
            dma((3,)), dma((3,)),
            dma((3, 8)), dma((3, 8)),
            dma((phases - 1, 2)), dma((phases - 1, 2)),
            dma((phases - 1, 4)), dma((phases - 1, 4)),
            dma((phases - 2, 2)), dma((phases - 2, 2)),
            dma((2,)), dma((2,)),
        ],
        compiler_params=pltpu.CompilerParams(
            collective_id=0, has_side_effects=True, vmem_limit_bytes=32 * 2**20),
    )(source, shift, start_field)


def solution(mesh):
    placed = P("blk", "narrow", None)
    return jax.shard_map(
        per_device, mesh=mesh, in_specs=(placed,) * 3, out_specs=placed, check_vma=False
    )
```

time: 262 us -> 73.8 us (0.28)
  starting transfers between devices: 140 us -> 0 us
  waiting for transfers between devices: 82.6 us -> 0 us
  Pallas kernels: 0 us -> 69.6 us
  other arithmetic: 25.5 us -> 0 us
  local copies, waits for them, and re-layouts: 10.3 us -> 3.92 us
    ppermute x58 -> x0, starting transfers between devices: 140 us -> none  [the longest x25 73.8 us: extended(): lax.ppermute(head, axis, [((i + 1) % count, i) for i in range(ends)])]
    ppermute x58 -> x0, waiting for transfers between devices: 82.6 us -> none  [the longest x25 54.8 us: extended(): lax.ppermute(head, axis, [((i + 1) % count, i) for i in range(ends)])]
    pallas_call x0 -> x1, Pallas kernels: none -> 69.6 us  [per_device(): pl.pallas_call(kernel, out_shape=jax.ShapeDtypeStruct(source.shape, sourc...]
    add x44 -> x0, other arithmetic: 10.8 us -> none  [the longest x16 5.24 us: smooth(): along_x = 0.5 * (padded[:-2] + padded[2:]) + padded[1:-1]]
    concatenate x16 -> x0, other arithmetic: 9.47 us -> none  [extended(): jnp.concatenate([lax.ppermute(tail, axis, [(i, (i + 1) % count) for i in...]
    mul x4 -> x0, other arithmetic: 3.35 us -> none  [per_device(): update = update * active]
    unnamed x23 -> x7, local copies, waits for them, and re-layouts: 7 us -> 3.92 us
  transfers between devices with their start and end apart: 58 -> 0, of which waited for: 31 -> 0; matrix products, arithmetic and copies ran while one was open for 1% -> 0% of each run, Pallas kernels for 0% -> 0%
where the time goes in v1:
time: 73.8 us; the launch traced here: 73.5 us
  Pallas kernels  69.6 us (94%)
  local copies, waits for them, and re-layouts  3.92 us (5%)
    pallas_call x1, Pallas kernels, per_device(): pl.pallas_call(kernel, out_shape=jax.ShapeDtypeStruct(source.shape, sourc...  69.6 us
    unnamed x7, local copies, waits for them, and re-layouts  3.92 us

profile of v1, /device:TPU:1, one launch (start us, length us, event | category | flops | bytes accessed | tf_op | source)
XLA Modules:
  0.0 73.5 jit_solution(17078487374729578305)
XLA Ops:
  0.0 0.0 copy-start
  0.0 1.0 %copy-done = f32[128,8,128]{2,1,0:T(8,128)S(1)} copy-done((f32[128,8,128]{2,1,0:T(8,128)S(1)}, f32[128,8,128]{2,1,0:T(8,128)}, u32[]{:S(2)}) %copy-start) | copy-done | bytes 524312
  1.0 0.0 copy-start.1
  1.0 1.0 %copy-done.1 = f32[128,8,128]{2,1,0:T(8,128)S(1)} copy-done((f32[128,8,128]{2,1,0:T(8,128)S(1)}, f32[128,8,128]{2,1,0:T(8,128)}, u32[]{:S(2)}) %copy-start.1) | copy-done | bytes 524312
  2.1 0.0 copy-start.2
  2.1 1.0 %copy-done.2 = f32[128,8,128]{2,1,0:T(8,128)S(1)} copy-done((f32[128,8,128]{2,1,0:T(8,128)S(1)}, f32[128,8,128]{2,1,0:T(8,128)}, u32[]{:S(2)}) %copy-start.2) | copy-done | bytes 524312
  3.1 69.6 %shard_map.37 = f32[128,8,128]{2,1,0:T(8,128)S(1)} custom-call(f32[128,8,128]{2,1,0:T(8,128)S(1)} %copy-done, f32[128,8,128]{2,1,0:T(8,128)S(1)} %copy-done.1, f32[128,8,128]{2,1,0:T(8,128)S(1)} %copy-done.2), custom_call_target="tpu_custom_call" | custom-call | tf_op jit(solution)/shard_map/pallas_call | solution.py:412
  72.7 0.8 %copy.5 = f32[128,8,128]{2,1,0:T(8,128)} copy(f32[128,8,128]{2,1,0:T(8,128)S(1)} %shard_map.37) | data formatting | bytes 1048576
Async XLA Ops:
  0.0 1.0 %copy-start = (f32[128,8,128]{2,1,0:T(8,128)S(1)}, f32[128,8,128]{2,1,0:T(8,128)}, u32[]{:S(2)}) copy-start(f32[128,8,128]{2,1,0:T(8,128)} %source.1) | copy-start | bytes 1572868
  1.0 1.0 %copy-start.1 = (f32[128,8,128]{2,1,0:T(8,128)S(1)}, f32[128,8,128]{2,1,0:T(8,128)}, u32[]{:S(2)}) copy-start(f32[128,8,128]{2,1,0:T(8,128)} %shift.1) | copy-start | bytes 1572868
  2.1 1.0 %copy-start.2 = (f32[128,8,128]{2,1,0:T(8,128)S(1)}, f32[128,8,128]{2,1,0:T(8,128)}, u32[]{:S(2)}) copy-start(f32[128,8,128]{2,1,0:T(8,128)} %start.1) | copy-start | bytes 1572868

commit v2 on v1

--- a/solution.py
+++ b/solution.py
@@ -9,7 +9,7 @@
 PASSES = 3
 SWEEPS = 2
 HALO = PASSES + 1
-UNROLL = 4
+UNROLL = 20
 MESH = pl.DeviceIdType.MESH
 
 low_end = 0.05
@@ -241,10 +241,12 @@
         pass_two(inner + 2, outer - 2)
         pass_three(inner + 3, outer - 3)
 
-    def solve_edges():
+    def solve_edge(side):
         for k, run in enumerate((residual, pass_one, pass_two, pass_three)):
-            run(1, inner + k)
-            run(outer - k, end)
+            if side == 0:
+                run(1, inner + k)
+            else:
+                run(outer - k, end)
 
     def across(e, side):
         dx = 1 if side == 0 else -1
@@ -286,9 +288,7 @@
             send_sem=last_send.at[side], recv_sem=last_recv.at[side],
             device_id=device(dx, 0), device_id_type=MESH)
 
-    def send_after(e):
-        for side in (0, 1):
-            across(e, side).start()
+    def send_halo(e):
         if e < 2 * SWEEPS - 2:
             for dy in (1, -1):
                 when_to(dy, along(e, dy).start)
@@ -310,23 +310,33 @@
             return carry
         lax.fori_loop(0, keep, body, 0)
 
-    def take_margins(e):
-        for side in (0, 1):
-            across(e, side).wait_recv()
-            for dy in (1, -1):
-                when_to(dy, forward(e, side, dy).start)
-        for side in (0, 1):
-            for dy in (1, -1):
-                when_from(dy, forward(e, side, dy).wait_recv)
-
-        def body(i, carry):
-            F[i] = X[2 * e, i]
-            F[base + n - OV + i] = X[2 * e + 1, i]
-            return carry
-        lax.fori_loop(0, edge, body, 0)
+    def send_side(e, side):
+        across(e, 1 - side).start()
+
+    def pass_margin_on(e, side):
+        across(e, side).wait_recv()
+        for dy in (1, -1):
+            when_to(dy, forward(e, side, dy).start)
+
+    def take_margin(e, side):
+        for dy in (1, -1):
+            when_from(dy, forward(e, side, dy).wait_recv)
+        begin = 0 if side == 0 else base + n - OV
+        for i in range(edge):
+            F[begin + i] = X[2 * e + side, i]
+
+    def margins_done(e):
         for side in (0, 1):
             for dy in (1, -1):
                 when_to(dy, forward(e, side, dy).wait_send)
+
+    def step(e, order, send):
+        for side in order:
+            pass_margin_on(e - 1, side)
+        for side in order:
+            take_margin(e - 1, side)
+            solve_edge(side)
+            send(side)
 
     def write_out(first, count, k):
         return pltpu.make_async_copy(
@@ -343,8 +353,10 @@
         all_initial(side_dirs, True, False)
         solve_inside()
         all_initial(cross_dirs, True, False)
-        solve_edges()
-        send_after(0)
+        for side in (0, 1):
+            solve_edge(side)
+            send_side(0, side)
+        send_halo(0)
         all_initial(side_dirs, True, False, True)
         all_initial(cross_dirs, False, False, True)
         for sweep in range(1, SWEEPS):
@@ -352,9 +364,9 @@
             finish_sends(e - 2)
             take_halo(e - 2)
             solve_inside()
-            take_margins(e - 1)
-            solve_edges()
-            send_after(e)
+            step(e, (0, 1), lambda side: send_side(e, side))
+            send_halo(e)
+            margins_done(e - 1)
         finish_sends(2 * SWEEPS - 2)
         middle = write_out(OV, n - 2 * OV, 0)
         middle.start()
@@ -390,12 +402,12 @@
                 finish_sends(e - 2)
                 take_halo(e - 2)
                 solve_inside()
-            take_margins(e - 1)
-            solve_edges()
             if sweep < SWEEPS - 1:
-                send_after(e)
-        for side in (0, 1):
-            last_copy(side).start()
+                step(e, (1, 0), lambda side: send_side(e, side))
+                send_halo(e)
+            else:
+                step(e, (1, 0), lambda side: last_copy(1 - side).start())
+            margins_done(e - 1)
         whole = write_out(0, n, 0)
         whole.start()
         for side in (0, 1):
@@ -425,7 +437,7 @@
             dma((2,)), dma((2,)),
         ],
         compiler_params=pltpu.CompilerParams(
-            collective_id=0, has_side_effects=True, vmem_limit_bytes=32 * 2**20),
+            collective_id=0, has_side_effects=True, vmem_limit_bytes=58 * 2**20),
     )(source, shift, start_field)
 
 

time: 73.8 us -> 51.3 us (0.70)
  Pallas kernels: 69.6 us -> 49.3 us
  local copies, waits for them, and re-layouts: 3.92 us -> 1.87 us
    pallas_call x1, Pallas kernels: 69.6 us -> 49.3 us  [per_device(): pl.pallas_call(kernel, out_shape=jax.ShapeDtypeStruct(source.shape, sourc...]
    unnamed x7 -> x1, local copies, waits for them, and re-layouts: 3.92 us -> 1.87 us
where the time goes in v2:
time: 51.3 us; the launch traced here: 51.2 us
  Pallas kernels  49.3 us (96%)
  local copies, waits for them, and re-layouts  1.87 us (4%)
    pallas_call x1, Pallas kernels, per_device(): pl.pallas_call(kernel, out_shape=jax.ShapeDtypeStruct(source.shape, sourc...  49.3 us
    unnamed x1, local copies, waits for them, and re-layouts  1.87 us

profile of v2, /device:TPU:1, one launch (start us, length us, event | category | flops | bytes accessed | tf_op | source)
XLA Modules:
  0.0 51.2 jit_solution(1985177301701431228)
XLA Ops:
  0.0 49.3 %shard_map.37 = f32[128,8,128]{2,1,0:T(8,128)} custom-call(f32[128,8,128]{2,1,0:T(8,128)} %source.1, f32[128,8,128]{2,1,0:T(8,128)} %shift.1, f32[128,8,128]{2,1,0:T(8,128)} %start.1), custom_call_target="tpu_custom_call" | custom-call | tf_op jit(solution)/shard_map/pallas_call | solution.py:424
  49.3 1.9 %copy.5 = f32[128,8,128]{2,1,0:T(8,128)} copy(f32[128,8,128]{2,1,0:T(8,128)} %shard_map.37) | data formatting | bytes 1048576

commit v3 on v2

--- a/solution.py
+++ b/solution.py
@@ -146,7 +146,8 @@
                 else:
                     when_from(dy, copy.wait_recv)
 
-    side_dirs, cross_dirs = (0, 1), (2, 3, 4, 5, 6, 7)
+    side_dirs, cross_dirs = (0, 1), (2, 4, 5, 3, 6, 7)
+    side_cross = (cross_dirs[:3], cross_dirs[3:])
 
     lane = lax.broadcasted_iota(jnp.int32, (8, nz), 1)
     first_lane, last_lane = lane == 0, lane == nz - 1
@@ -352,8 +353,8 @@
             copy.wait()
         all_initial(side_dirs, True, False)
         solve_inside()
-        all_initial(cross_dirs, True, False)
-        for side in (0, 1):
+        for side in (0, 1):
+            all_initial(side_cross[side], True, False)
             solve_edge(side)
             send_side(0, side)
         send_halo(0)
@@ -388,7 +389,8 @@
 
     @pl.when(odd)
     def _():
-        all_initial(cross_dirs, True, True)
+        for side in (0, 1):
+            all_initial(side_cross[side], True, True)
         for copy in own:
             copy.wait()
         all_initial(side_dirs, True, False)

time: 51.3 us -> 51.3 us (level)
  no operation moved by 1% of the time
where the time goes in v3:
time: 51.3 us; the launch traced here: 51.2 us
  Pallas kernels  49.3 us (96%)
  local copies, waits for them, and re-layouts  1.87 us (4%)
    pallas_call x1, Pallas kernels, per_device(): pl.pallas_call(kernel, out_shape=jax.ShapeDtypeStruct(source.shape, sourc...  49.3 us
    unnamed x1, local copies, waits for them, and re-layouts  1.87 us

profile of v3, /device:TPU:1, one launch (start us, length us, event | category | flops | bytes accessed | tf_op | source)
XLA Modules:
  0.0 51.2 jit_solution(3333594409531448786)
XLA Ops:
  0.0 49.3 %shard_map.37 = f32[128,8,128]{2,1,0:T(8,128)} custom-call(f32[128,8,128]{2,1,0:T(8,128)} %source.1, f32[128,8,128]{2,1,0:T(8,128)} %shift.1, f32[128,8,128]{2,1,0:T(8,128)} %start.1), custom_call_target="tpu_custom_call" | custom-call | tf_op jit(solution)/shard_map/pallas_call | solution.py:426
  49.3 1.9 %copy.5 = f32[128,8,128]{2,1,0:T(8,128)} copy(f32[128,8,128]{2,1,0:T(8,128)} %shard_map.37) | data formatting | bytes 1048576
